TPU v7x, 128 devices: a whole 4x4x4 slice. The times are simulated.
128 devices in a mesh: fsdp: 8 (over y, x_lo), row: 4 (over x_hi, core), col: 4 (over z).
Axes of the slice: x: 4 (x_hi: 2, x_lo: 2; x = x_hi * 2 + x_lo), y: 4, z: 4, core: 2. Of those that a mesh axis runs over, the one named last changes fastest.
Arguments:
- grad: bfloat16 [8, 1024, 16384], P(None, 'fsdp', ('row', 'col')), may hold values from -6 to 6
- momentum: float32 [8, 1024, 16384], P(None, 'fsdp', ('row', 'col')), may hold values from -6 to 6
- variance: float32 [8, 1024, 16384], P(None, 'fsdp', ('row', 'col')), may hold values from 0.05 to 4
- weight: bfloat16 [8, 1024, 16384], P(None, 'fsdp', ('row', 'col')), may hold values from -6 to 6
- left_inverse: float32 [8, 1024, 1024], P('row', ('fsdp', 'col')), may hold values from -1 to 4, as said below
- right_inverse: float32 [4, 4, 1024, 1024], P(None, 'col', ('fsdp', 'row')), may hold values from -1 to 4, as said below
Outputs:
- momentum_next: float32 [8, 1024, 16384], P(None, 'fsdp', ('row', 'col'))
- variance_next: float32 [8, 1024, 16384], P(None, 'fsdp', ('row', 'col'))
- weight_next: bfloat16 [8, 1024, 16384], P(None, 'fsdp', ('row', 'col'))
Inputs may be any that keep to these rules, and one draw needn't show every extreme that they name: `left_inverse`: each block is symmetric positive definite. `right_inverse`: each block is symmetric positive definite.
All inputs are finite; a program needn't handle non-finite values.
Results may differ from a plain program's by a relative error of at most 0.001.
Values sent between devices are 32-bit elements; how exact they have to be, the bound alone decides.
A program may use at most 128 MiB of HBM per device.

v0:
```python
import jax
import jax.numpy as jnp
from jax import lax
from jax.sharding import Mesh
from jax.sharding import PartitionSpec as P

FSDP_ROW = ("fsdp_0", "fsdp_1", "row")
FSDP = ("fsdp_0", "fsdp_1")
FSDP_COL = ("fsdp_0", "fsdp_1", "col")


first_decay = 0.9
second_decay = 0.95
learn_rate = 0.1
weight_decay = 0.1
epsilon = 1e-08


def split_up(x, dim, count):
    shape = x.shape
    pieces = x.reshape(*shape[:dim], count, shape[dim] // count, *shape[dim + 1 :])
    return jnp.moveaxis(pieces, dim, 0)


def joined_along(pieces, dim):
    shape = list(pieces.shape[1:])
    shape[dim] *= pieces.shape[0]
    return jnp.moveaxis(pieces, 0, dim).reshape(shape)


def one_exchange(x, axis, axes, splits, concats):
    sizes = [lax.axis_size(a) for a in axes]
    pieces = split_up(x, splits[0], sizes[0])
    pieces = jnp.moveaxis(split_up(pieces, splits[1] + 1, sizes[1]), 0, 1)
    inside = pieces.shape[2:]
    pieces = pieces.reshape(-1, *inside)
    pieces = lax.all_to_all(pieces, axis, split_axis=0, concat_axis=0, tiled=True)
    pieces = joined_along(pieces.reshape(*sizes, *inside), concats[0] + 1)
    return joined_along(pieces, concats[1])


def gather_axes(x, axes, dim):
    for axis in reversed(axes):
        x = lax.all_gather(x, axis, axis=dim, tiled=True)
    return x


def per_device(grad, momentum, variance, weight, left_inverse, right_inverse):
    highest = lax.Precision.HIGHEST
    momentum_next = first_decay * momentum + (1.0 - first_decay) * grad.astype(jnp.float32)
    relayed = lax.all_to_all(
        lax.all_to_all(momentum_next, FSDP, split_axis=2, concat_axis=1, tiled=True),
        "row",
        split_axis=0,
        concat_axis=2,
        tiled=True,
    )
    mixed = jnp.einsum(
        "kij,kjn->kin",
        lax.all_gather(left_inverse, FSDP_COL, axis=1, tiled=True),
        relayed,
        precision=highest,
        preferred_element_type=jnp.float32,
    )
    groups = lax.axis_size("row")
    grouped = mixed.reshape(mixed.shape[0], mixed.shape[1], groups, mixed.shape[2] // groups)
    own_rows_block = lax.all_to_all(right_inverse, "row", split_axis=0, concat_axis=2, tiled=True)
    back_tiles = one_exchange(grouped, FSDP_ROW, (FSDP, "row"), (1, 2), (3, 0))
    tiles = back_tiles.reshape(momentum.shape)
    precond = jnp.einsum(
        "kip,pn->kin",
        tiles,
        gather_axes(own_rows_block, FSDP, 2)[0, 0],
        precision=highest,
        preferred_element_type=jnp.float32,
    )
    variance_next = second_decay * variance + (1.0 - second_decay) * precond * precond
    weight_float = weight.astype(jnp.float32)
    weight_next = weight_float - learn_rate * (
        precond / (jnp.sqrt(variance_next) + epsilon) + weight_decay * weight_float
    )
    return (momentum_next, variance_next, weight_next.astype(jnp.bfloat16))


def solution(mesh):
    torus = Mesh(
        mesh.devices.reshape(4, 2, mesh.shape["row"], mesh.shape["col"]),
        ("fsdp_0", "fsdp_1", "row", "col"),
    )
    in_specs = (
        P(None, FSDP, ("row", "col")),
        P(None, FSDP, ("row", "col")),
        P(None, FSDP, ("row", "col")),
        P(None, FSDP, ("row", "col")),
        P("row", FSDP_COL, None),
        P(None, "col", FSDP_ROW, None),
    )
    out_specs = (
        P(None, FSDP, ("row", "col")),
        P(None, FSDP, ("row", "col")),
        P(None, FSDP, ("row", "col")),
    )
    return jax.shard_map(
        per_device, mesh=torus, in_specs=in_specs, out_specs=out_specs, check_vma=False
    )
```

profile of v0, /device:TPU:1, one launch (start us, length us, event | category | flops | bytes accessed | tf_op | source)
XLA Modules:
  0.0 370.0 jit_solution(14506037472035503490)
XLA Ops:
  7.2 0.0 all-gather.6.cloned.1.call-start
  7.2 15.2 %all_to_all.53 = f32[4,1,32,1024]{3,2,1,0:T(8,128)} all-to-all(f32[4,1,32,1024]{3,2,1,0:T(8,128)} %param.11), channel_id=1, replica_groups=mesh['fsdp_0'=4,'fsdp_1'=2,'row'=4,'col'=4] {'row'}, dimensions={0} | all-to-all | bytes 1048576 | tf_op jit(solution)/shard_map/all_to_all | solution.py:67
  22.4 0.0 all-gather.6.cloned.1.call-update
  22.5 0.0 all-gather.4.cloned.1.call-start
  22.5 0.7 all-gather.4.cloned.1.call-update
  23.2 5.9 %multiply_add_fusion = f32[8,128,1024]{2,1,0:T(8,128)} fusion(bf16[8,128,1024]{2,1,0:T(8,128)(2,1)} %param.6, f32[8,128,1024]{2,1,0:T(8,128)} %param.7), kind=kLoop, calls=%fused_computation.9 | loop fusion | flops 4194304 | bytes 10485760 | tf_op jit(solution)/shard_map/add | solution.py:50
  29.1 5.4 %copy.18 = f32[8,128,1024]{1,0,2:T(8,128)} copy(f32[8,128,1024]{2,1,0:T(8,128)} %multiply_add_fusion) | data formatting | bytes 8388608 | tf_op jit(solution)/shard_map/add | solution.py:50
  34.5 84.5 %all_to_all.54 = f32[8,128,1024]{1,0,2:T(8,128)} all-to-all(f32[8,128,1024]{1,0,2:T(8,128)} %copy.18), channel_id=1, replica_groups=mesh['fsdp_0'=4,'fsdp_1'=2,'row'=4,'col'=4] {'fsdp_0','fsdp_1'}, dimensions={2} | all-to-all | bytes 8388608 | tf_op jit(solution)/shard_map/all_to_all | solution.py:52
  119.0 5.4 %copy.20 = f32[8,8,128,128]{3,2,1,0:T(8,128)} copy(f32[8,8,128,128]{2,0,3,1:T(8,128)} %bitcast.43) | data formatting | bytes 8388608 | tf_op jit(solution)/shard_map/all_to_all | solution.py:52
  124.4 6.8 %all-to-all-start.1 = ((f32[8,1024,128]{2,1,0:T(8,128)}), f32[8,1024,128]{2,1,0:T(8,128)}, u32[]{:S(2)}, u32[]{:S(2)}) async-start(f32[8,1024,128]{2,1,0:T(8,128)} %bitcast.42), calls=%async_computation.1 | async-start | bytes 8388608 | tf_op jit(solution)/shard_map/all_to_all | solution.py:51
  131.2 0.0 all-gather.8.cloned.1.call-start
  131.2 0.0 all-gather.6.cloned.1.call-done
  131.2 0.7 all-gather.8.cloned.1.call-update
  132.0 92.9 %all-to-all-done.1 = f32[8,1024,128]{2,1,0:T(8,128)} async-done(((f32[8,1024,128]{2,1,0:T(8,128)}), f32[8,1024,128]{2,1,0:T(8,128)}, u32[]{:S(2)}, u32[]{:S(2)}) %all-to-all-start.1) | async-done | bytes 4194336 | tf_op jit(solution)/shard_map/all_to_all | solution.py:51
  224.8 5.4 %copy.21 = f32[2,1024,4,128]{1,3,2,0:T(8,128)} copy(f32[2,1024,4,128]{3,1,0,2:T(8,128)} %bitcast.5) | data formatting | bytes 8388608 | tf_op jit(solution)/shard_map/all_to_all | solution.py:51
  230.2 8.1 %all-gather.4.cloned.1.call-done = f32[2,1024,1024]{2,1,0:T(8,128)} async-done(((f32[2,32,1024]{2,1,0:T(8,128)}), f32[2,1024,1024]{2,1,0:T(8,128)}) %all-gather.4.cloned.1.call-update) | async-done | bytes 8388624 | tf_op jit(solution)/shard_map/all_gather | solution.py:60
  238.3 16.7 %fusion.7 = f32[2,512,1024]{2,1,0:T(8,128)S(1)} fusion(f32[2,1024,512]{1,2,0:T(8,128)} %bitcast.47, f32[2,1024,1024]{2,1,0:T(8,128)} %all-gather.4.cloned.1.call-done), kind=kOutput, calls=%fused_computation.10 | convolution fusion | flops 12884901888 | bytes 16777216 | tf_op jit(solution)/shard_map/kij,kjn->kin/dot_general | solution.py:58
  255.1 3.0 copy.26
  258.1 5.3 %copy.22 = f32[2,8,128,4,128]{4,2,0,3,1:T(8,128)} copy(f32[2,8,128,4,128]{2,1,4,3,0:T(8,128)} %bitcast.44) | data formatting | bytes 8388608 | tf_op jit(solution)/shard_map/reshape;reshape | solution.py:21
  263.4 70.7 %all_to_all.55 = f32[32,2,128,1,128]{4,2,1,3,0:T(8,128)S(1)} all-to-all(f32[32,2,128,1,128]{4,2,1,3,0:T(8,128)} %bitcast.45), channel_id=1, replica_groups=mesh['fsdp_0'=4,'fsdp_1'=2,'row'=4,'col'=4] {'fsdp_0','fsdp_1','row'}, dimensions={0} | all-to-all | bytes 8388608 | tf_op jit(solution)/shard_map/all_to_all | solution.py:37
  334.1 4.4 %copy.24 = f32[4,2,128,1,8,128]{5,4,2,1,0,3:T(8,128)} copy(f32[4,2,128,1,8,128]{5,2,1,0,4,3:T(8,128)S(1)} %bitcast.46) | data formatting | bytes 8388608 | tf_op jit(solution)/shard_map/transpose | solution.py:28
  338.5 0.0 copy-start
  338.5 5.1 %reshape_reshape_reshape.3 = f32[8,128,1024]{2,1,0:T(8,128)} reshape(f32[4,2,128,1,8,128]{5,4,2,1,0,3:T(8,128)} %copy.24) | data formatting | bytes 8388608 | tf_op jit(solution)/shard_map/reshape;reshape;reshape | solution.py:69
  343.5 0.0 all-gather.8.cloned.1.call-done
  343.5 0.0 copy-done
  343.5 20.0 %fusion.2 = (bf16[8,128,1024]{2,1,0:T(8,128)(2,1)}, f32[8,128,1024]{2,1,0:T(8,128)}) fusion(bf16[8,128,1024]{2,1,0:T(8,128)(2,1)S(1)} %copy-done, f32[8,128,1024]{2,1,0:T(8,128)} %param.8, f32[8,128,1024]{2,1,0:T(8,128)} %reshape_reshape_reshape.3, f32[1,1,1024,1024]{3,2,1,0:T(8,128)} %all-gather.8.cloned.1.call-done), kind=kOutput, calls=%fused_computation.5 | convolution fusion | flops 12897484800 | bytes 20971520 | tf_op jit(solution)/shard_map/kip,pn->kin/dot_general | solution.py:70
Async XLA Ops:
  7.2 124.1 %all-gather.6.cloned.1.call-start = ((), (), s32[]{:S(2)}) async-start(), calls=%async_computation.5 | async-start | bytes 1572864 | tf_op jit(solution)/shard_map/all_gather | solution.py:44
  22.5 215.9 %all-gather.4.cloned.1.call-start = ((), (), s32[]{:S(2)}) async-start(), calls=%async_computation.4 | async-start | bytes 8650752 | tf_op jit(solution)/shard_map/all_gather | solution.py:60
  124.4 100.4 %all-to-all-start.1 = ((f32[8,1024,128]{2,1,0:T(8,128)}), f32[8,1024,128]{2,1,0:T(8,128)}, u32[]{:S(2)}, u32[]{:S(2)}) async-start(f32[8,1024,128]{2,1,0:T(8,128)} %bitcast.42), calls=%async_computation.1 | async-start | bytes 8388608 | tf_op jit(solution)/shard_map/all_to_all | solution.py:51
  131.2 212.3 %all-gather.8.cloned.1.call-start = ((), (), s32[]{:S(2)}) async-start(), calls=%async_computation.6 | async-start | bytes 5242880 | tf_op jit(solution)/shard_map/all_gather | solution.py:44
  338.5 5.1 %copy-start = (bf16[8,128,1024]{2,1,0:T(8,128)(2,1)S(1)}, bf16[8,128,1024]{2,1,0:T(8,128)(2,1)}, u32[]{:S(2)}) copy-start(bf16[8,128,1024]{2,1,0:T(8,128)(2,1)} %param.9) | copy-start | bytes 6291460
Sparse Core Ops, SparseCore 0:
  22.6 29.1 all-gather.5
  53.5 184.8 all-gather.3
  240.0 97.0 all-gather.7
where the time goes:
time: 371 us; the launch traced here: 370 us
  blocking collectives  170 us (46%)
  waiting for transfers between devices  102 us (27%)
  matrix products  36.7 us (10%)
  local copies, waits for them, and re-layouts  33.8 us (9%)
  between operations  13.8 us (4%)
  starting transfers between devices  6.92 us (2%)
  other arithmetic  5.92 us (2%)
    all_to_all x1, waiting for transfers between devices, per_device(): lax.all_to_all(lax.all_to_all(momentum_next, FSDP, split_axis=2, concat_a...  92.9 us
    all_to_all x1, blocking collectives, per_device(): lax.all_to_all(momentum_next, FSDP, split_axis=2, concat_axis=1, tiled=True)  84.5 us
    all_to_all x1, blocking collectives, one_exchange(): lax.all_to_all(pieces, axis, split_axis=0, concat_axis=0, tiled=True)  70.7 us
    dot_general x1, matrix products, per_device(): jnp.einsum('kip,pn->kin', tiles, gather_axes(own_rows_block, FSDP, 2)[0,...  20 us
    dot_general x1, matrix products, per_device(): jnp.einsum('kij,kjn->kin', lax.all_gather(left_inverse, FSDP_COL, axis=1,...  16.7 us
    all_to_all x1, blocking collectives, per_device(): lax.all_to_all(right_inverse, 'row', split_axis=0, concat_axis=2, tiled=T...  15.2 us
    all_gather x1, waiting for transfers between devices, per_device(): lax.all_gather(left_inverse, FSDP_COL, axis=1, tiled=True)  8.14 us
  transfers between devices with their start and end apart: 4, of which 2 were waited for; matrix products, arithmetic and copies ran while one was open for 15% of the time, Pallas kernels for 0%

commit v1 on v0

v1 whole, which is shorter than its diff:
```python
import functools

import jax
import jax.numpy as jnp
from jax import lax
from jax.experimental import pallas as pl
from jax.experimental.pallas import tpu as pltpu
from jax.sharding import Mesh
from jax.sharding import PartitionSpec as P

AXES = ("y", "a", "h", "k", "z")
MESH = pl.DeviceIdType.MESH

first_decay = 0.9
second_decay = 0.95
learn_rate = 0.1
weight_decay = 0.1
epsilon = 1e-08

PARTS = 4
WIDE = 1024 // PARTS


def split(x):
    high = x.astype(jnp.bfloat16)
    low = (x - high.astype(jnp.float32)).astype(jnp.bfloat16)
    return high, low


def product(left_high, left_low, right_high, right_low):
    dot = functools.partial(jnp.dot, preferred_element_type=jnp.float32)
    return dot(left_high, right_high) + (dot(left_high, right_low) + dot(left_low, right_high))


def kernel(
    grad, momentum, left, right, out,
    grad_in, own, tile, left_all, right_all, left_hi, left_lo, right_hi, right_lo,
    tile_hi, tile_lo, mixed_hi, mixed_lo, done,
    in_sem, own_send, own_recv, l1_send, l1_recv, l2_send, l2_recv, l3_send, l3_recv,
    r1_send, r1_recv, r2_send, r2_recv, r3_send, r3_recv, p_send, p_recv,
):
    y, a, h, k, z = (lax.axis_index(name) for name in AXES)
    me_f = 2 * y + a

    def remote(src, dst, send, recv, device):
        return pltpu.make_async_remote_copy(
            src_ref=src, dst_ref=dst, send_sem=send, recv_sem=recv, device_id=device, device_id_type=MESH
        )

    def arrived(dst, recv):
        pltpu.make_async_copy(dst, dst, recv).wait()

    loads = []
    for b in range(8):
        pair = (
            pltpu.make_async_copy(momentum.at[b], own.at[b], in_sem.at[0, b]),
            pltpu.make_async_copy(grad.at[b], grad_in.at[b], in_sem.at[1, b]),
        )
        for copy in pair:
            copy.start()
        loads.append(pair)

    barrier = pltpu.get_barrier_semaphore()
    others = []
    for dy in range(4):
        for da in range(2):
            for dk in range(2):
                if (dy, da, dk) != (0, 0, 0):
                    others.append((lax.rem(y + dy, 4), lax.rem(a + da, 2), h, lax.rem(k + dk, 2), z))
    for da in range(2):
        others.append((y, lax.rem(a + da, 2), 1 - h, k, z))
    for dz in range(1, 4):
        others.append((y, a, h, k, lax.rem(z + dz, 4)))
    for device in others:
        pl.semaphore_signal(barrier, inc=1, device_id=device, device_id_type=MESH)
    pl.semaphore_wait(barrier, len(others))

    home = 2 * h + k
    holder = h == y // 2
    for t in range(2):
        stays = jnp.logical_and(y == home, k == t)

        @pl.when(stays)
        def _():
            pltpu.make_async_copy(left.at[t], left_all.at[y, a, z], l1_recv.at[y]).start()

        @pl.when(jnp.logical_not(stays))
        def _():
            remote(
                left.at[t], left_all.at[y, a, z], l1_send.at[t], l1_recv.at[y], (home, a, h, jnp.int32(t), z)
            ).start()

    def r1(i):
        to_a, to_h = lax.rem(a + i % 2, 2), lax.rem(h + i // 2, 2)
        return remote(
            right.at[2 * to_h + to_a, 0], right_all.at[y, a, h, k], r1_send.at[i], r1_recv.at[i], (y, to_a, to_h, k, z)
        )

    pltpu.make_async_copy(right.at[2 * h + a, 0], right_all.at[y, a, h, k], r1_recv.at[0]).start()
    for i in range(1, 4):
        r1(i).start()

    def own_part(dy, t, part):
        to_y = lax.rem(y + dy, 4)
        columns = pl.ds(part * WIDE, WIDE)
        return (
            own.at[2 * to_y + t, :, columns],
            tile.at[me_f, :, columns],
            own_send.at[dy, t, part],
            own_recv.at[me_f, part],
            (to_y, k, h, jnp.int32(t), z),
        )

    for b in range(8):
        for copy in loads[b]:
            copy.wait()
        own[b] = first_decay * own[b] + (1.0 - first_decay) * grad_in[b].astype(jnp.float32)
    for part in range(PARTS):
        for dy in (2, 1, 3, 0):
            for t in range(2):
                src, dst, send, recv, device = own_part(dy, t, part)
                if dy == 0:
                    stays = jnp.logical_and(a == k, k == t)

                    @pl.when(stays)
                    def _():
                        pltpu.make_async_copy(src, dst, recv).start()

                    @pl.when(jnp.logical_not(stays))
                    def _():
                        remote(src, dst, send, recv, device).start()
                else:
                    remote(src, dst, send, recv, device).start()

    for i in range(4):
        arrived(right_all.at[y, lax.rem(a + i % 2, 2), lax.rem(h + i // 2, 2), k], r1_recv.at[i])

    def r2(dy):
        rows = right_all.at[y, :, :, k]
        return remote(rows, rows, r2_send.at[dy - 1], r2_recv.at[dy - 1], (lax.rem(y + dy, 4), a, h, k, z))

    def r3(dy):
        rows = right_all.at[lax.rem(y - dy + 4, 4), :, :, k]
        return remote(rows, rows, r3_send.at[dy], r3_recv.at[dy], (y, a, h, 1 - k, z))

    for dy in (2, 1, 3):
        r2(dy).start()
    r3(0).start()

    def l2(i):
        rows = left_all.at[:, a, z]
        device = (y, lax.rem(a + i % 2, 2), lax.rem(h + i // 2, 2), k, z)
        return remote(rows, rows, l2_send.at[i - 1], l2_recv.at[a], device)

    @pl.when(holder)
    def _():
        for from_y in range(4):
            arrived(left_all.at[from_y, a, z], l1_recv.at[from_y])
        for i in range(1, 4):
            l2(i).start()

    def l3(i, dz):
        rows = left_all.at[:, lax.rem(a + i, 2), z]
        return remote(rows, rows, l3_send.at[i, dz - 1], l3_recv.at[lax.rem(a + i, 2), dz - 1],
                      (y, a, h, k, lax.rem(z + dz, 4)))

    for i in range(2):
        from_a = lax.rem(a + i, 2)
        if i == 0:

            @pl.when(jnp.logical_not(holder))
            def _():
                arrived(left_all.at[:, from_a, z], l2_recv.at[from_a])
        else:
            arrived(left_all.at[:, from_a, z], l2_recv.at[from_a])
        for dz in (2, 1, 3):
            l3(i, dz).start()

    for dy in (1, 3, 2):
        from_y = lax.rem(y - dy + 4, 4)
        arrived(right_all.at[from_y, :, :, k], r2_recv.at[dy - 1])
        r3(dy).start()

    def split_left(from_z):
        for f in range(8):
            high, low = split(left_all[f // 2, f % 2, from_z])
            rows = pl.ds(pl.multiple_of(f * 128 + from_z * 32, 32), 32)
            left_hi[rows], left_lo[rows] = high, low

    split_left(z)
    for dz in (1, 3, 2):
        from_z = lax.rem(z - dz + 4, 4)
        for from_a in range(2):
            arrived(left_all.at[:, from_a, from_z], l3_recv.at[from_a, dz - 1])
        split_left(from_z)

    for part in range(PARTS):
        columns = slice(part * WIDE, (part + 1) * WIDE)
        for f in range(8):
            arrived(tile.at[f, :, columns], own_recv.at[f, part])

        @pl.loop(0, 8)
        def _(f):
            rows = pl.ds(pl.multiple_of(f * 128, 128), 128)
            tile_hi[rows], tile_lo[rows] = split(tile[f, :, columns])

        @pl.loop(0, 4)
        def _(i):
            rows = pl.ds(pl.multiple_of(i * 256, 256), 256)
            mixed = product(left_hi[rows], left_lo[rows], tile_hi[...], tile_lo[...])
            mixed_hi[rows, columns], mixed_lo[rows, columns] = split(mixed)

    for dy in (0, 1, 3, 2):
        arrived(right_all.at[lax.rem(y - dy + 4, 4), :, :, 1 - k], r3_recv.at[dy])

    @pl.loop(0, 32)
    def _(i):
        rows = pl.ds(pl.multiple_of(i * 32, 32), 32)
        right_hi[rows], right_lo[rows] = split(right_all[i // 8, (i // 4) % 2, (i // 2) % 2, i % 2])

    def p_copy(dy, to_a):
        to_y = lax.rem(y + dy, 4)
        return (done.at[2 * to_y + to_a], out.at[2 * y + k], p_send.at[dy, to_a], p_recv.at[2 * y + k],
                (to_y, jnp.int32(to_a), h, a, z))

    for dy in (2, 1, 3, 0):
        to_y = lax.rem(y + dy, 4)
        rows = pl.ds(pl.multiple_of(to_y * 256, 256), 256)

        @pl.loop(0, 4)
        def _(i):
            columns = pl.ds(pl.multiple_of(i * 256, 256), 256)
            both = product(mixed_hi[rows], mixed_lo[rows], right_hi[:, columns], right_lo[:, columns])
            done[2 * to_y, :, columns] = both[:128]
            done[2 * to_y + 1, :, columns] = both[128:]

        for to_a in range(2):
            src, dst, send, recv, device = p_copy(dy, to_a)
            if dy == 0:
                stays = jnp.logical_and(a == k, a == to_a)

                @pl.when(stays)
                def _():
                    pltpu.make_async_copy(src, dst, recv).start()

                @pl.when(jnp.logical_not(stays))
                def _():
                    remote(src, dst, send, recv, device).start()
            else:
                remote(src, dst, send, recv, device).start()

    for t in range(2):

        @pl.when(jnp.logical_not(jnp.logical_and(y == home, k == t)))
        def _():
            remote(
                left.at[t], left_all.at[y, a, z], l1_send.at[t], l1_recv.at[y], (home, a, h, jnp.int32(t), z)
            ).wait_send()

    for i in range(1, 4):
        r1(i).wait_send()

    @pl.when(holder)
    def _():
        for i in range(1, 4):
            l2(i).wait_send()

    for i in range(2):
        for dz in range(1, 4):
            l3(i, dz).wait_send()
    for dy in range(1, 4):
        r2(dy).wait_send()
    for dy in range(4):
        r3(dy).wait_send()
    for dy in range(4):
        for t in range(2):
            sends = [remote(*own_part(dy, t, part)) for part in range(PARTS)] + [remote(*p_copy(dy, t))]
            if dy == 0:

                @pl.when(jnp.logical_not(jnp.logical_and(a == k, k == t)))
                def _():
                    for copy in sends:
                        copy.wait_send()
            else:
                for copy in sends:
                    copy.wait_send()
    for b in range(8):
        arrived(out.at[b], p_recv.at[b])


def precondition(grad, momentum, left, right):
    f32, bf16 = jnp.float32, jnp.bfloat16
    dma = pltpu.SemaphoreType.DMA
    return pl.pallas_call(
        kernel,
        out_shape=jax.ShapeDtypeStruct((8, 128, 1024), f32),
        in_specs=[pl.BlockSpec(memory_space=pl.ANY)] * 4,
        out_specs=pl.BlockSpec(memory_space=pl.ANY),
        scratch_shapes=[
            pltpu.VMEM((8, 128, 1024), bf16),
            pltpu.VMEM((8, 128, 1024), f32),
            pltpu.VMEM((8, 128, 1024), f32),
            pltpu.VMEM((4, 2, 4, 32, 1024), f32),
            pltpu.VMEM((4, 2, 2, 2, 32, 1024), f32),
            pltpu.VMEM((1024, 1024), bf16),
            pltpu.VMEM((1024, 1024), bf16),
            pltpu.VMEM((1024, 1024), bf16),
            pltpu.VMEM((1024, 1024), bf16),
            pltpu.VMEM((1024, WIDE), bf16),
            pltpu.VMEM((1024, WIDE), bf16),
            pltpu.VMEM((1024, 1024), bf16),
            pltpu.VMEM((1024, 1024), bf16),
            pltpu.VMEM((8, 128, 1024), f32),
            dma((2, 8)),
            dma((4, 2, PARTS)), dma((8, PARTS)),
            dma((2,)), dma((4,)), dma((3,)), dma((2,)), dma((2, 3)), dma((2, 3)),
            dma((4,)), dma((4,)), dma((3,)), dma((3,)), dma((4,)), dma((4,)),
            dma((4, 2)), dma((8,)),
        ],
        compiler_params=pltpu.CompilerParams(
            collective_id=0, has_side_effects=True, vmem_limit_bytes=56 * 2**20
        ),
        cost_estimate=pl.CostEstimate(flops=3 * 2**32, bytes_accessed=20 * 2**20, transcendentals=0),
    )(grad, momentum, left, right)


def per_device(grad, momentum, variance, weight, left_inverse, right_inverse):
    precond = precondition(grad, momentum, left_inverse, right_inverse)
    momentum_next = first_decay * momentum + (1.0 - first_decay) * grad.astype(jnp.float32)
    variance_next = second_decay * variance + (1.0 - second_decay) * precond * precond
    weight_float = weight.astype(jnp.float32)
    weight_next = weight_float - learn_rate * (
        precond / (jnp.sqrt(variance_next) + epsilon) + weight_decay * weight_float
    )
    return (momentum_next, variance_next, weight_next.astype(jnp.bfloat16))


def solution(mesh):
    torus = Mesh(mesh.devices.reshape(4, 2, 2, 2, 4), AXES)
    tiles = P(None, ("y", "a"), ("h", "k", "z"))
    in_specs = (
        tiles,
        tiles,
        tiles,
        tiles,
        P(("h", "k"), ("y", "a", "z"), None),
        P(None, "z", ("y", "a", "h", "k"), None),
    )
    return jax.shard_map(
        per_device, mesh=torus, in_specs=in_specs, out_specs=(tiles, tiles, tiles), check_vma=False
    )
```

time: 371 us -> 179 us (0.48)
  the two profiles are of different devices: /device:TPU:1 before, /device:TPU:101 now
where the time goes in v1:
time: 179 us
  Pallas kernels  170 us (95%)
  other arithmetic  8.92 us (5%)
    pallas_call x1, Pallas kernels, precondition(): pl.pallas_call(kernel, out_shape=jax.ShapeDtypeStruct((8, 128, 1024), f32...  170 us
    convert_element_type x1, other arithmetic, per_device(): return (momentum_next, variance_next, weight_next.astype(jnp.bfloat16))  6.11 us

profile of v1, /device:TPU:101, one launch (start us, length us, event | category | flops | bytes accessed | tf_op | source)
XLA Modules:
  0.0 179.2 jit_solution(4965522667220863513)
XLA Ops:
  0.6 0.0 copy-start.3
  0.6 0.0 copy-start.1
  0.7 169.6 %shard_map.85 = f32[8,128,1024]{2,1,0:T(8,128)} custom-call(bf16[8,128,1024]{2,1,0:T(8,128)(2,1)} %grad.1, f32[8,128,1024]{2,1,0:T(8,128)} %momentum.1, f32[2,32,1024]{2,1,0:T(8,128)} %left.1, f32[4,1,32,1024]{3,2,1,0:T(8,128)} %right.1), custom_call_target="tpu_custom_call" | custom-call | flops 12884901888 | bytes 20971520 | tf_op jit(solution)/shard_map/pallas_call | solution.py:294
  170.3 0.0 copy-done.3
  170.3 0.0 copy-done.1
  170.3 0.0 copy-start
  170.3 0.0 copy-start.2
  170.3 6.1 %fusion.2 = (bf16[8,128,1024]{2,1,0:T(8,128)(2,1)}, f32[8,128,1024]{2,1,0:T(8,128)}) fusion(bf16[8,128,1024]{2,1,0:T(8,128)(2,1)S(1)} %copy-done.3, f32[8,128,1024]{2,1,0:T(8,128)} %shard_map.85, f32[8,128,1024]{2,1,0:T(8,128)S(1)} %copy-done.1), kind=kLoop, calls=%fused_computation.5 | loop fusion | flops 12582912 | bytes 16777216 | tf_op jit(solution)/shard_map/convert_element_type | solution.py:335
  176.4 0.0 copy-done
  176.4 0.0 copy-done.2
  176.4 2.8 %multiply_add_fusion = f32[8,128,1024]{2,1,0:T(8,128)} fusion(bf16[8,128,1024]{2,1,0:T(8,128)(2,1)S(1)} %copy-done.2, f32[8,128,1024]{2,1,0:T(8,128)S(1)} %copy-done), kind=kLoop, calls=%fused_computation.7 | loop fusion | flops 4194304 | bytes 10485760 | tf_op jit(solution)/shard_map/add | solution.py:329
Async XLA Ops:
  0.6 169.6 %copy-start.3 = (bf16[8,128,1024]{2,1,0:T(8,128)(2,1)S(1)}, bf16[8,128,1024]{2,1,0:T(8,128)(2,1)}, u32[]{:S(2)}) copy-start(bf16[8,128,1024]{2,1,0:T(8,128)(2,1)} %param.9) | copy-start | bytes 6291460
  0.6 169.6 %copy-start.1 = (f32[8,128,1024]{2,1,0:T(8,128)S(1)}, f32[8,128,1024]{2,1,0:T(8,128)}, u32[]{:S(2)}) copy-start(f32[8,128,1024]{2,1,0:T(8,128)} %param.8) | copy-start | bytes 12582916
  170.3 6.1 %copy-start = (f32[8,128,1024]{2,1,0:T(8,128)S(1)}, f32[8,128,1024]{2,1,0:T(8,128)}, u32[]{:S(2)}) copy-start(f32[8,128,1024]{2,1,0:T(8,128)} %momentum.1) | copy-start | bytes 12582916
  170.3 6.1 %copy-start.2 = (bf16[8,128,1024]{2,1,0:T(8,128)(2,1)S(1)}, bf16[8,128,1024]{2,1,0:T(8,128)(2,1)}, u32[]{:S(2)}) copy-start(bf16[8,128,1024]{2,1,0:T(8,128)(2,1)} %grad.1) | copy-start | bytes 6291460

commit v2 on v1

--- a/solution.py
+++ b/solution.py
@@ -19,6 +19,7 @@
 
 PARTS = 4
 WIDE = 1024 // PARTS
+KEPT = 5
 
 
 def split(x):
@@ -34,14 +35,17 @@
 
 def kernel(
     grad, momentum, left, right, out,
-    grad_in, own, tile, left_all, right_all, left_hi, left_lo, right_hi, right_lo,
+    grad_in, own, tile, left_own, right_own, left_all, right_all, left_hi, left_lo, right_hi, right_lo,
     tile_hi, tile_lo, mixed_hi, mixed_lo, done,
-    in_sem, own_send, own_recv, l1_send, l1_recv, l2_send, l2_recv, l3_send, l3_recv,
-    r1_send, r1_recv, r2_send, r2_recv, r3_send, r3_recv, p_send, p_recv,
+    in_sem, pack_sem, own_send, own_recv, l1_send, l1_recv, l2_send, l2_recv, l3_send, l3_recv, l4_send, l4_recv,
+    r1_send, r1_recv, r2_send, r2_recv, r3_send, r3_recv, r4_send, r4_recv, p_send, p_recv,
 ):
     y, a, h, k, z = (lax.axis_index(name) for name in AXES)
     me_f = 2 * y + a
 
+    def step(at, by):
+        return lax.rem(at + by + 4, 4)
+
     def remote(src, dst, send, recv, device):
         return pltpu.make_async_remote_copy(
             src_ref=src, dst_ref=dst, send_sem=send, recv_sem=recv, device_id=device, device_id_type=MESH
@@ -50,6 +54,14 @@
     def arrived(dst, recv):
         pltpu.make_async_copy(dst, dst, recv).wait()
 
+    packs = []
+    for d in range(KEPT):
+        columns = pl.ds(pl.multiple_of(lax.rem(me_f + d, 8) * 128, 128), 128)
+        packed = pl.ds(d * 128, 128)
+        packs.append(pltpu.make_async_copy(left.at[:, :, columns], left_own.at[:, :, packed], pack_sem.at[0, d]))
+        packs.append(pltpu.make_async_copy(right.at[:, 0, :, columns], right_own.at[:, :, packed], pack_sem.at[1, d]))
+    for copy in packs:
+        copy.start()
     loads = []
     for b in range(8):
         pair = (
@@ -66,42 +78,48 @@
         for da in range(2):
             for dk in range(2):
                 if (dy, da, dk) != (0, 0, 0):
-                    others.append((lax.rem(y + dy, 4), lax.rem(a + da, 2), h, lax.rem(k + dk, 2), z))
+                    others.append((step(y, dy), lax.rem(a + da, 2), h, lax.rem(k + dk, 2), z))
     for da in range(2):
         others.append((y, lax.rem(a + da, 2), 1 - h, k, z))
     for dz in range(1, 4):
-        others.append((y, a, h, k, lax.rem(z + dz, 4)))
+        others.append((y, a, h, k, step(z, dz)))
     for device in others:
         pl.semaphore_signal(barrier, inc=1, device_id=device, device_id_type=MESH)
+    for copy in packs:
+        copy.wait()
     pl.semaphore_wait(barrier, len(others))
 
     home = 2 * h + k
     holder = h == y // 2
+
+    def l1(t):
+        return remote(
+            left_own.at[t], left_all.at[y, a, z], l1_send.at[t], l1_recv.at[y], (home, a, h, jnp.int32(t), z)
+        )
+
     for t in range(2):
         stays = jnp.logical_and(y == home, k == t)
 
         @pl.when(stays)
         def _():
-            pltpu.make_async_copy(left.at[t], left_all.at[y, a, z], l1_recv.at[y]).start()
+            pltpu.make_async_copy(left_own.at[t], left_all.at[y, a, z], l1_recv.at[y]).start()
 
         @pl.when(jnp.logical_not(stays))
         def _():
-            remote(
-                left.at[t], left_all.at[y, a, z], l1_send.at[t], l1_recv.at[y], (home, a, h, jnp.int32(t), z)
-            ).start()
+            l1(t).start()
 
     def r1(i):
         to_a, to_h = lax.rem(a + i % 2, 2), lax.rem(h + i // 2, 2)
         return remote(
-            right.at[2 * to_h + to_a, 0], right_all.at[y, a, h, k], r1_send.at[i], r1_recv.at[i], (y, to_a, to_h, k, z)
-        )
-
-    pltpu.make_async_copy(right.at[2 * h + a, 0], right_all.at[y, a, h, k], r1_recv.at[0]).start()
+            right_own.at[2 * to_h + to_a], right_all.at[y, a, h, k], r1_send.at[i], r1_recv.at[i], (y, to_a, to_h, k, z)
+        )
+
+    pltpu.make_async_copy(right_own.at[2 * h + a], right_all.at[y, a, h, k], r1_recv.at[0]).start()
     for i in range(1, 4):
         r1(i).start()
 
     def own_part(dy, t, part):
-        to_y = lax.rem(y + dy, 4)
+        to_y = step(y, dy)
         columns = pl.ds(part * WIDE, WIDE)
         return (
             own.at[2 * to_y + t, :, columns],
@@ -111,11 +129,7 @@
             (to_y, k, h, jnp.int32(t), z),
         )
 
-    for b in range(8):
-        for copy in loads[b]:
-            copy.wait()
-        own[b] = first_decay * own[b] + (1.0 - first_decay) * grad_in[b].astype(jnp.float32)
-    for part in range(PARTS):
+    def send_part(part):
         for dy in (2, 1, 3, 0):
             for t in range(2):
                 src, dst, send, recv, device = own_part(dy, t, part)
@@ -132,20 +146,11 @@
                 else:
                     remote(src, dst, send, recv, device).start()
 
-    for i in range(4):
-        arrived(right_all.at[y, lax.rem(a + i % 2, 2), lax.rem(h + i // 2, 2), k], r1_recv.at[i])
-
-    def r2(dy):
-        rows = right_all.at[y, :, :, k]
-        return remote(rows, rows, r2_send.at[dy - 1], r2_recv.at[dy - 1], (lax.rem(y + dy, 4), a, h, k, z))
-
-    def r3(dy):
-        rows = right_all.at[lax.rem(y - dy + 4, 4), :, :, k]
-        return remote(rows, rows, r3_send.at[dy], r3_recv.at[dy], (y, a, h, 1 - k, z))
-
-    for dy in (2, 1, 3):
-        r2(dy).start()
-    r3(0).start()
+    for b in range(8):
+        for copy in loads[b]:
+            copy.wait()
+        own[b] = first_decay * own[b] + (1.0 - first_decay) * grad_in[b].astype(jnp.float32)
+    send_part(0)
 
     def l2(i):
         rows = left_all.at[:, a, z]
@@ -156,13 +161,37 @@
     def _():
         for from_y in range(4):
             arrived(left_all.at[from_y, a, z], l1_recv.at[from_y])
-        for i in range(1, 4):
+        for i in (2, 3, 1):
             l2(i).start()
 
-    def l3(i, dz):
-        rows = left_all.at[:, lax.rem(a + i, 2), z]
-        return remote(rows, rows, l3_send.at[i, dz - 1], l3_recv.at[lax.rem(a + i, 2), dz - 1],
-                      (y, a, h, k, lax.rem(z + dz, 4)))
+    def r2(s):
+        rows = right_all.at[y, :, :, k]
+        return remote(rows, rows, r2_send.at[s], r2_recv.at[s], (step(y, 1 - 2 * s), a, h, k, z))
+
+    def r3(dy):
+        rows = right_all.at[step(y, -dy), :, :, k]
+        return remote(rows, rows, r3_send.at[dy], r3_recv.at[dy], (y, a, h, 1 - k, z))
+
+    def r4(s):
+        rows = right_all.at[step(y, 2 * s - 1), s, :, k]
+        return remote(rows, rows, r4_send.at[s], r4_recv.at[s], (step(y, 1 - 2 * s), a, h, k, z))
+
+    for i in range(4):
+        arrived(right_all.at[y, lax.rem(a + i % 2, 2), lax.rem(h + i // 2, 2), k], r1_recv.at[i])
+    for s in range(2):
+        r2(s).start()
+    r3(0).start()
+    for part in range(1, PARTS):
+        send_part(part)
+
+    def l3(i, s):
+        from_a = lax.rem(a + i, 2)
+        rows = left_all.at[:, from_a, z]
+        return remote(rows, rows, l3_send.at[i, s], l3_recv.at[from_a, s], (y, a, h, k, step(z, 1 - 2 * s)))
+
+    def l4(s):
+        rows = left_all.at[:, s, step(z, 2 * s - 1)]
+        return remote(rows, rows, l4_send.at[s], l4_recv.at[s], (y, a, h, k, step(z, 1 - 2 * s)))
 
     for i in range(2):
         from_a = lax.rem(a + i, 2)
@@ -173,26 +202,35 @@
                 arrived(left_all.at[:, from_a, z], l2_recv.at[from_a])
         else:
             arrived(left_all.at[:, from_a, z], l2_recv.at[from_a])
-        for dz in (2, 1, 3):
-            l3(i, dz).start()
-
-    for dy in (1, 3, 2):
-        from_y = lax.rem(y - dy + 4, 4)
-        arrived(right_all.at[from_y, :, :, k], r2_recv.at[dy - 1])
-        r3(dy).start()
-
-    def split_left(from_z):
-        for f in range(8):
-            high, low = split(left_all[f // 2, f % 2, from_z])
-            rows = pl.ds(pl.multiple_of(f * 128 + from_z * 32, 32), 32)
-            left_hi[rows], left_lo[rows] = high, low
-
-    split_left(z)
-    for dz in (1, 3, 2):
-        from_z = lax.rem(z - dz + 4, 4)
-        for from_a in range(2):
-            arrived(left_all.at[:, from_a, from_z], l3_recv.at[from_a, dz - 1])
-        split_left(from_z)
+        for s in range(2):
+            l3(i, s).start()
+
+    for s in range(2):
+        arrived(right_all.at[step(y, 2 * s - 1), :, :, k], r2_recv.at[s])
+        r4(s).start()
+        r3(1 + 2 * s).start()
+    for s in range(2):
+        arrived(left_all.at[:, s, step(z, 2 * s - 1)], l3_recv.at[s, s])
+        l4(s).start()
+    for s in range(2):
+        arrived(right_all.at[step(y, 2), s, :, k], r4_recv.at[s])
+    r3(2).start()
+    for s in range(2):
+        arrived(left_all.at[:, 1 - s, step(z, 2 * s - 1)], l3_recv.at[1 - s, s])
+        arrived(left_all.at[:, s, step(z, 2)], l4_recv.at[s])
+
+    def unpack(rows_of, high, low):
+        @pl.loop(0, 8)
+        def _(f):
+            at = pl.ds(pl.multiple_of(f * 128, 128), 128)
+            for d in range(KEPT):
+                block = rows_of(f, pl.ds(d * 128, 128)).reshape(128, 128)
+                to = pl.ds(pl.multiple_of(lax.rem(f + d, 8) * 128, 128), 128)
+                high[at, to], low[at, to] = split(block)
+                if 0 < d < 4:
+                    high[to, at], low[to, at] = split(block.T)
+
+    unpack(lambda f, c: left_all[f // 2, lax.rem(f, 2), :, :, c], left_hi, left_lo)
 
     for part in range(PARTS):
         columns = slice(part * WIDE, (part + 1) * WIDE)
@@ -210,21 +248,18 @@
             mixed = product(left_hi[rows], left_lo[rows], tile_hi[...], tile_lo[...])
             mixed_hi[rows, columns], mixed_lo[rows, columns] = split(mixed)
 
-    for dy in (0, 1, 3, 2):
-        arrived(right_all.at[lax.rem(y - dy + 4, 4), :, :, 1 - k], r3_recv.at[dy])
-
-    @pl.loop(0, 32)
-    def _(i):
-        rows = pl.ds(pl.multiple_of(i * 32, 32), 32)
-        right_hi[rows], right_lo[rows] = split(right_all[i // 8, (i // 4) % 2, (i // 2) % 2, i % 2])
+        if part == max(PARTS - 2, 0):
+            for dy in (0, 1, 3, 2):
+                arrived(right_all.at[step(y, -dy), :, :, 1 - k], r3_recv.at[dy])
+            unpack(lambda f, c: right_all[f // 2, lax.rem(f, 2), :, :, :, c], right_hi, right_lo)
 
     def p_copy(dy, to_a):
-        to_y = lax.rem(y + dy, 4)
+        to_y = step(y, dy)
         return (done.at[2 * to_y + to_a], out.at[2 * y + k], p_send.at[dy, to_a], p_recv.at[2 * y + k],
                 (to_y, jnp.int32(to_a), h, a, z))
 
     for dy in (2, 1, 3, 0):
-        to_y = lax.rem(y + dy, 4)
+        to_y = step(y, dy)
         rows = pl.ds(pl.multiple_of(to_y * 256, 256), 256)
 
         @pl.loop(0, 4)
@@ -253,9 +288,7 @@
 
         @pl.when(jnp.logical_not(jnp.logical_and(y == home, k == t)))
         def _():
-            remote(
-                left.at[t], left_all.at[y, a, z], l1_send.at[t], l1_recv.at[y], (home, a, h, jnp.int32(t), z)
-            ).wait_send()
+            l1(t).wait_send()
 
     for i in range(1, 4):
         r1(i).wait_send()
@@ -265,11 +298,12 @@
         for i in range(1, 4):
             l2(i).wait_send()
 
-    for i in range(2):
-        for dz in range(1, 4):
-            l3(i, dz).wait_send()
-    for dy in range(1, 4):
-        r2(dy).wait_send()
+    for s in range(2):
+        l3(0, s).wait_send()
+        l3(1, s).wait_send()
+        l4(s).wait_send()
+        r2(s).wait_send()
+        r4(s).wait_send()
     for dy in range(4):
         r3(dy).wait_send()
     for dy in range(4):
@@ -300,8 +334,10 @@
             pltpu.VMEM((8, 128, 1024), bf16),
             pltpu.VMEM((8, 128, 1024), f32),
             pltpu.VMEM((8, 128, 1024), f32),
-            pltpu.VMEM((4, 2, 4, 32, 1024), f32),
-            pltpu.VMEM((4, 2, 2, 2, 32, 1024), f32),
+            pltpu.VMEM((2, 32, KEPT * 128), f32),
+            pltpu.VMEM((4, 32, KEPT * 128), f32),
+            pltpu.VMEM((4, 2, 4, 32, KEPT * 128), f32),
+            pltpu.VMEM((4, 2, 2, 2, 32, KEPT * 128), f32),
             pltpu.VMEM((1024, 1024), bf16),
             pltpu.VMEM((1024, 1024), bf16),
             pltpu.VMEM((1024, 1024), bf16),
@@ -311,10 +347,10 @@
             pltpu.VMEM((1024, 1024), bf16),
             pltpu.VMEM((1024, 1024), bf16),
             pltpu.VMEM((8, 128, 1024), f32),
-            dma((2, 8)),
+            dma((2, 8)), dma((2, KEPT)),
             dma((4, 2, PARTS)), dma((8, PARTS)),
-            dma((2,)), dma((4,)), dma((3,)), dma((2,)), dma((2, 3)), dma((2, 3)),
-            dma((4,)), dma((4,)), dma((3,)), dma((3,)), dma((4,)), dma((4,)),
+            dma((2,)), dma((4,)), dma((3,)), dma((2,)), dma((2, 2)), dma((2, 2)), dma((2,)), dma((2,)),
+            dma((4,)), dma((4,)), dma((2,)), dma((2,)), dma((4,)), dma((4,)), dma((2,)), dma((2,)),
             dma((4, 2)), dma((8,)),
         ],
         compiler_params=pltpu.CompilerParams(

time: 179 us -> 136 us (0.76)
  the two profiles are of different devices: /device:TPU:101 before, /device:TPU:1 now
where the time goes in v2:
time: 136 us
  Pallas kernels  126 us (93%)
  other arithmetic  8.92 us (7%)
    pallas_call x1, Pallas kernels, precondition(): pl.pallas_call(kernel, out_shape=jax.ShapeDtypeStruct((8, 128, 1024), f32...  126 us
    convert_element_type x1, other arithmetic, per_device(): return (momentum_next, variance_next, weight_next.astype(jnp.bfloat16))  6.11 us
    add x1, other arithmetic, per_device(): first_decay * momentum + (1.0 - first_decay) * grad.astype(jnp.float32)  2.81 us

profile of v2, /device:TPU:1, one launch (start us, length us, event | category | flops | bytes accessed | tf_op | source)
XLA Modules:
  0.0 136.0 jit_solution(489214436208452326)
XLA Ops:
  0.6 0.0 copy-start.3
  0.6 0.0 copy-start.1
  0.7 126.4 %shard_map.85 = f32[8,128,1024]{2,1,0:T(8,128)} custom-call(bf16[8,128,1024]{2,1,0:T(8,128)(2,1)} %grad.1, f32[8,128,1024]{2,1,0:T(8,128)} %momentum.1, f32[2,32,1024]{2,1,0:T(8,128)} %left.1, f32[4,1,32,1024]{3,2,1,0:T(8,128)} %right.1), custom_call_target="tpu_custom_call" | custom-call | flops 12884901888 | bytes 20971520 | tf_op jit(solution)/shard_map/pallas_call | solution.py:328
  127.0 0.0 copy-done.3
  127.1 0.0 copy-done.1
  127.1 0.0 copy-start
  127.1 0.0 copy-start.2
  127.1 6.1 %fusion.2 = (bf16[8,128,1024]{2,1,0:T(8,128)(2,1)}, f32[8,128,1024]{2,1,0:T(8,128)}) fusion(bf16[8,128,1024]{2,1,0:T(8,128)(2,1)S(1)} %copy-done.3, f32[8,128,1024]{2,1,0:T(8,128)} %shard_map.85, f32[8,128,1024]{2,1,0:T(8,128)S(1)} %copy-done.1), kind=kLoop, calls=%fused_computation.5 | loop fusion | flops 12582912 | bytes 16777216 | tf_op jit(solution)/shard_map/convert_element_type | solution.py:371
  133.2 0.0 copy-done
  133.2 0.0 copy-done.2
  133.2 2.8 %multiply_add_fusion = f32[8,128,1024]{2,1,0:T(8,128)} fusion(bf16[8,128,1024]{2,1,0:T(8,128)(2,1)S(1)} %copy-done.2, f32[8,128,1024]{2,1,0:T(8,128)S(1)} %copy-done), kind=kLoop, calls=%fused_computation.7 | loop fusion | flops 4194304 | bytes 10485760 | tf_op jit(solution)/shard_map/add | solution.py:365
Async XLA Ops:
  0.6 126.4 %copy-start.3 = (bf16[8,128,1024]{2,1,0:T(8,128)(2,1)S(1)}, bf16[8,128,1024]{2,1,0:T(8,128)(2,1)}, u32[]{:S(2)}) copy-start(bf16[8,128,1024]{2,1,0:T(8,128)(2,1)} %param.9) | copy-start | bytes 6291460
  0.6 126.4 %copy-start.1 = (f32[8,128,1024]{2,1,0:T(8,128)S(1)}, f32[8,128,1024]{2,1,0:T(8,128)}, u32[]{:S(2)}) copy-start(f32[8,128,1024]{2,1,0:T(8,128)} %param.8) | copy-start | bytes 12582916
  127.1 6.1 %copy-start = (f32[8,128,1024]{2,1,0:T(8,128)S(1)}, f32[8,128,1024]{2,1,0:T(8,128)}, u32[]{:S(2)}) copy-start(f32[8,128,1024]{2,1,0:T(8,128)} %momentum.1) | copy-start | bytes 12582916
  127.1 6.1 %copy-start.2 = (bf16[8,128,1024]{2,1,0:T(8,128)(2,1)S(1)}, bf16[8,128,1024]{2,1,0:T(8,128)(2,1)}, u32[]{:S(2)}) copy-start(bf16[8,128,1024]{2,1,0:T(8,128)(2,1)} %grad.1) | copy-start | bytes 6291460

commit v3 on v2

--- a/solution.py
+++ b/solution.py
@@ -19,6 +19,8 @@
 
 PARTS = 4
 WIDE = 1024 // PARTS
+HOME_PARTS = 2
+HOME_WIDE = 1024 // HOME_PARTS
 KEPT = 5
 
 
@@ -34,10 +36,10 @@
 
 
 def kernel(
-    grad, momentum, left, right, out,
-    grad_in, own, tile, left_own, right_own, left_all, right_all, left_hi, left_lo, right_hi, right_lo,
+    grad, momentum, variance, weight, left, right, own, variance_out, weight_out,
+    grad_in, home_tile, tile, left_own, right_own, left_all, right_all, left_hi, left_lo, right_hi, right_lo,
     tile_hi, tile_lo, mixed_hi, mixed_lo, done,
-    in_sem, pack_sem, own_send, own_recv, l1_send, l1_recv, l2_send, l2_recv, l3_send, l3_recv, l4_send, l4_recv,
+    in_sem, pack_sem, late_sem, own_send, own_recv, l1_send, l1_recv, l2_send, l2_recv, l3_send, l3_recv, l4_send, l4_recv,
     r1_send, r1_recv, r2_send, r2_recv, r3_send, r3_recv, r4_send, r4_recv, p_send, p_recv,
 ):
     y, a, h, k, z = (lax.axis_index(name) for name in AXES)
@@ -71,6 +73,13 @@
         for copy in pair:
             copy.start()
         loads.append(pair)
+    late = [
+        pltpu.make_async_copy(variance, variance_out, late_sem.at[0]),
+        pltpu.make_async_copy(weight, weight_out, late_sem.at[1]),
+    ]
+
+    for copy in late:
+        copy.start()
 
     barrier = pltpu.get_barrier_semaphore()
     others = []
@@ -85,7 +94,16 @@
         others.append((y, a, h, k, step(z, dz)))
     for device in others:
         pl.semaphore_signal(barrier, inc=1, device_id=device, device_id_type=MESH)
-    for copy in packs:
+    for b in range(8):
+        for copy in loads[b]:
+            copy.wait()
+
+        @pl.loop(0, 4)
+        def _(i):
+            rows = pl.ds(pl.multiple_of(i * 32, 32), 32)
+            own[b, rows] = first_decay * own[b, rows] + (1.0 - first_decay) * grad_in[b, rows].astype(jnp.float32)
+
+    for copy in packs + late:
         copy.wait()
     pl.semaphore_wait(barrier, len(others))
 
@@ -146,23 +164,32 @@
                 else:
                     remote(src, dst, send, recv, device).start()
 
-    for b in range(8):
-        for copy in loads[b]:
-            copy.wait()
-        own[b] = first_decay * own[b] + (1.0 - first_decay) * grad_in[b].astype(jnp.float32)
     send_part(0)
 
-    def l2(i):
-        rows = left_all.at[:, a, z]
+    def l2(i, from_y):
+        rows = left_all.at[from_y, a, z]
         device = (y, lax.rem(a + i % 2, 2), lax.rem(h + i // 2, 2), k, z)
-        return remote(rows, rows, l2_send.at[i - 1], l2_recv.at[a], device)
+        return remote(rows, rows, l2_send.at[i - 1, from_y], l2_recv.at[a, from_y], device)
+
+    def l3(from_a, s, from_y):
+        rows = left_all.at[from_y, from_a, z]
+        return remote(
+            rows, rows, l3_send.at[from_a, s, from_y], l3_recv.at[from_a, s, from_y], (y, a, h, k, step(z, 1 - 2 * s))
+        )
+
+    def l4(s, from_y):
+        rows = left_all.at[from_y, s, step(z, 2 * s - 1)]
+        return remote(rows, rows, l4_send.at[s, from_y], l4_recv.at[s, from_y], (y, a, h, k, step(z, 1 - 2 * s)))
 
     @pl.when(holder)
     def _():
-        for from_y in range(4):
+        for dy in (0, 1, 3, 2):
+            from_y = step(y, dy)
             arrived(left_all.at[from_y, a, z], l1_recv.at[from_y])
-        for i in (2, 3, 1):
-            l2(i).start()
+            for i in (2, 3, 1):
+                l2(i, from_y).start()
+            for s in range(2):
+                l3(a, s, from_y).start()
 
     def r2(s):
         rows = right_all.at[y, :, :, k]
@@ -181,43 +208,38 @@
     for s in range(2):
         r2(s).start()
     r3(0).start()
-    for part in range(1, PARTS):
+    send_part(1)
+    for dy in (0, 1, 3, 2):
+        from_y = step(y, dy)
+
+        @pl.when(jnp.logical_not(holder))
+        def _():
+            arrived(left_all.at[from_y, a, z], l2_recv.at[a, from_y])
+            for s in range(2):
+                l3(a, s, from_y).start()
+
+        arrived(left_all.at[from_y, 1 - a, z], l2_recv.at[1 - a, from_y])
+        for s in range(2):
+            l3(1 - a, s, from_y).start()
+    for part in range(2, PARTS):
         send_part(part)
-
-    def l3(i, s):
-        from_a = lax.rem(a + i, 2)
-        rows = left_all.at[:, from_a, z]
-        return remote(rows, rows, l3_send.at[i, s], l3_recv.at[from_a, s], (y, a, h, k, step(z, 1 - 2 * s)))
-
-    def l4(s):
-        rows = left_all.at[:, s, step(z, 2 * s - 1)]
-        return remote(rows, rows, l4_send.at[s], l4_recv.at[s], (y, a, h, k, step(z, 1 - 2 * s)))
-
-    for i in range(2):
-        from_a = lax.rem(a + i, 2)
-        if i == 0:
-
-            @pl.when(jnp.logical_not(holder))
-            def _():
-                arrived(left_all.at[:, from_a, z], l2_recv.at[from_a])
-        else:
-            arrived(left_all.at[:, from_a, z], l2_recv.at[from_a])
-        for s in range(2):
-            l3(i, s).start()
 
     for s in range(2):
         arrived(right_all.at[step(y, 2 * s - 1), :, :, k], r2_recv.at[s])
         r4(s).start()
         r3(1 + 2 * s).start()
-    for s in range(2):
-        arrived(left_all.at[:, s, step(z, 2 * s - 1)], l3_recv.at[s, s])
-        l4(s).start()
+    for dy in (0, 1, 3, 2):
+        for s in range(2):
+            from_y = step(y, dy)
+            arrived(left_all.at[from_y, s, step(z, 2 * s - 1)], l3_recv.at[s, s, from_y])
+            l4(s, from_y).start()
     for s in range(2):
         arrived(right_all.at[step(y, 2), s, :, k], r4_recv.at[s])
     r3(2).start()
     for s in range(2):
-        arrived(left_all.at[:, 1 - s, step(z, 2 * s - 1)], l3_recv.at[1 - s, s])
-        arrived(left_all.at[:, s, step(z, 2)], l4_recv.at[s])
+        for from_y in range(4):
+            arrived(left_all.at[from_y, 1 - s, step(z, 2 * s - 1)], l3_recv.at[1 - s, s, from_y])
+            arrived(left_all.at[from_y, s, step(z, 2)], l4_recv.at[s, from_y])
 
     def unpack(rows_of, high, low):
         @pl.loop(0, 8)
@@ -232,8 +254,16 @@
 
     unpack(lambda f, c: left_all[f // 2, lax.rem(f, 2), :, :, c], left_hi, left_lo)
 
+    def left_rows(rows, columns):
+        mixed = product(left_hi[rows], left_lo[rows], tile_hi[...], tile_lo[...])
+        mixed_hi[rows, columns], mixed_lo[rows, columns] = split(mixed)
+
     for part in range(PARTS):
         columns = slice(part * WIDE, (part + 1) * WIDE)
+        if part == PARTS - 1:
+            for dy in (0, 1, 3, 2):
+                arrived(right_all.at[step(y, -dy), :, :, 1 - k], r3_recv.at[dy])
+            unpack(lambda f, c: right_all[f // 2, lax.rem(f, 2), :, :, :, c], right_hi, right_lo)
         for f in range(8):
             arrived(tile.at[f, :, columns], own_recv.at[f, part])
 
@@ -242,47 +272,69 @@
             rows = pl.ds(pl.multiple_of(f * 128, 128), 128)
             tile_hi[rows], tile_lo[rows] = split(tile[f, :, columns])
 
-        @pl.loop(0, 4)
-        def _(i):
-            rows = pl.ds(pl.multiple_of(i * 256, 256), 256)
-            mixed = product(left_hi[rows], left_lo[rows], tile_hi[...], tile_lo[...])
-            mixed_hi[rows, columns], mixed_lo[rows, columns] = split(mixed)
-
-        if part == max(PARTS - 2, 0):
-            for dy in (0, 1, 3, 2):
-                arrived(right_all.at[step(y, -dy), :, :, 1 - k], r3_recv.at[dy])
-            unpack(lambda f, c: right_all[f // 2, lax.rem(f, 2), :, :, :, c], right_hi, right_lo)
-
-    def p_copy(dy, to_a):
+        if part < PARTS - 1:
+
+            @pl.loop(0, 4)
+            def _(i):
+                left_rows(pl.ds(pl.multiple_of(i * 256, 256), 256), columns)
+
+    def p_copy(dy, to_a, part):
         to_y = step(y, dy)
-        return (done.at[2 * to_y + to_a], out.at[2 * y + k], p_send.at[dy, to_a], p_recv.at[2 * y + k],
-                (to_y, jnp.int32(to_a), h, a, z))
+        columns = pl.ds(part * HOME_WIDE, HOME_WIDE)
+        return (
+            done.at[2 * to_y + to_a, :, columns],
+            home_tile.at[2 * y + k, :, columns],
+            p_send.at[dy, to_a, part],
+            p_recv.at[2 * y + k, part],
+            (to_y, jnp.int32(to_a), h, a, z),
+        )
 
     for dy in (2, 1, 3, 0):
         to_y = step(y, dy)
         rows = pl.ds(pl.multiple_of(to_y * 256, 256), 256)
-
-        @pl.loop(0, 4)
-        def _(i):
-            columns = pl.ds(pl.multiple_of(i * 256, 256), 256)
-            both = product(mixed_hi[rows], mixed_lo[rows], right_hi[:, columns], right_lo[:, columns])
-            done[2 * to_y, :, columns] = both[:128]
-            done[2 * to_y + 1, :, columns] = both[128:]
-
-        for to_a in range(2):
-            src, dst, send, recv, device = p_copy(dy, to_a)
-            if dy == 0:
-                stays = jnp.logical_and(a == k, a == to_a)
-
-                @pl.when(stays)
-                def _():
-                    pltpu.make_async_copy(src, dst, recv).start()
-
-                @pl.when(jnp.logical_not(stays))
-                def _():
+        left_rows(rows, columns)
+        for part in range(HOME_PARTS):
+
+            @pl.loop(0, HOME_WIDE // 256)
+            def _(i):
+                here = pl.ds(pl.multiple_of(part * HOME_WIDE + i * 256, 256), 256)
+                both = product(mixed_hi[rows], mixed_lo[rows], right_hi[:, here], right_lo[:, here])
+                done[2 * to_y, :, here] = both[:128]
+                done[2 * to_y + 1, :, here] = both[128:]
+
+            for to_a in range(2):
+                src, dst, send, recv, device = p_copy(dy, to_a, part)
+                if dy == 0:
+                    stays = jnp.logical_and(a == k, a == to_a)
+
+                    @pl.when(stays)
+                    def _():
+                        pltpu.make_async_copy(src, dst, recv).start()
+
+                    @pl.when(jnp.logical_not(stays))
+                    def _():
+                        remote(src, dst, send, recv, device).start()
+                else:
                     remote(src, dst, send, recv, device).start()
-            else:
-                remote(src, dst, send, recv, device).start()
+
+    for dy in (2, 1, 3, 0):
+        for t in range(2):
+            b = 2 * step(y, -dy) + t
+            for part in range(HOME_PARTS):
+                columns = pl.ds(part * HOME_WIDE, HOME_WIDE)
+                arrived(home_tile.at[b, :, columns], p_recv.at[b, part])
+
+            @pl.loop(0, 8)
+            def _(i):
+                rows = pl.ds(pl.multiple_of(i * 16, 16), 16)
+                precond = home_tile[b, rows]
+                variance_next = second_decay * variance_out[b, rows] + (1.0 - second_decay) * precond * precond
+                weight_float = weight_out[b, rows].astype(jnp.float32)
+                weight_next = weight_float - learn_rate * (
+                    precond / (jnp.sqrt(variance_next) + epsilon) + weight_decay * weight_float
+                )
+                variance_out[b, rows] = variance_next
+                weight_out[b, rows] = weight_next.astype(jnp.bfloat16)
 
     for t in range(2):
 
@@ -296,19 +348,22 @@
     @pl.when(holder)
     def _():
         for i in range(1, 4):
-            l2(i).wait_send()
+            for from_y in range(4):
+                l2(i, from_y).wait_send()
 
     for s in range(2):
-        l3(0, s).wait_send()
-        l3(1, s).wait_send()
-        l4(s).wait_send()
+        for from_y in range(4):
+            l3(0, s, from_y).wait_send()
+            l3(1, s, from_y).wait_send()
+            l4(s, from_y).wait_send()
         r2(s).wait_send()
         r4(s).wait_send()
     for dy in range(4):
         r3(dy).wait_send()
     for dy in range(4):
         for t in range(2):
-            sends = [remote(*own_part(dy, t, part)) for part in range(PARTS)] + [remote(*p_copy(dy, t))]
+            sends = [remote(*own_part(dy, t, part)) for part in range(PARTS)]
+            sends += [remote(*p_copy(dy, t, part)) for part in range(HOME_PARTS)]
             if dy == 0:
 
                 @pl.when(jnp.logical_not(jnp.logical_and(a == k, k == t)))
@@ -318,18 +373,30 @@
             else:
                 for copy in sends:
                     copy.wait_send()
-    for b in range(8):
-        arrived(out.at[b], p_recv.at[b])
-
-
-def precondition(grad, momentum, left, right):
+def store(momentum, variance, weight, momentum_out, variance_out, weight_out, sem):
+    copies = [
+        pltpu.make_async_copy(src.at[pl.ds(2 * i, 2)], dst.at[pl.ds(2 * i, 2)], sem.at[n, i])
+        for i in range(4)
+        for n, (src, dst) in enumerate(((momentum, momentum_out), (variance, variance_out), (weight, weight_out)))
+    ]
+    for copy in copies:
+        copy.start()
+    for copy in copies:
+        copy.wait()
+
+
+def update(grad, momentum, variance, weight, left, right):
     f32, bf16 = jnp.float32, jnp.bfloat16
     dma = pltpu.SemaphoreType.DMA
-    return pl.pallas_call(
+    updated = pl.pallas_call(
         kernel,
-        out_shape=jax.ShapeDtypeStruct((8, 128, 1024), f32),
-        in_specs=[pl.BlockSpec(memory_space=pl.ANY)] * 4,
-        out_specs=pl.BlockSpec(memory_space=pl.ANY),
+        out_shape=(
+            pltpu.VMEM((8, 128, 1024), f32),
+            pltpu.VMEM((8, 128, 1024), f32),
+            pltpu.VMEM((8, 128, 1024), bf16),
+        ),
+        in_specs=[pl.BlockSpec(memory_space=pl.ANY)] * 6,
+        out_specs=(pl.BlockSpec(memory_space=pltpu.VMEM),) * 3,
         scratch_shapes=[
             pltpu.VMEM((8, 128, 1024), bf16),
             pltpu.VMEM((8, 128, 1024), f32),
@@ -347,28 +414,25 @@
             pltpu.VMEM((1024, 1024), bf16),
             pltpu.VMEM((1024, 1024), bf16),
             pltpu.VMEM((8, 128, 1024), f32),
-            dma((2, 8)), dma((2, KEPT)),
+            dma((2, 8)), dma((2, KEPT)), dma((2,)),
             dma((4, 2, PARTS)), dma((8, PARTS)),
-            dma((2,)), dma((4,)), dma((3,)), dma((2,)), dma((2, 2)), dma((2, 2)), dma((2,)), dma((2,)),
+            dma((2,)), dma((4,)), dma((3, 4)), dma((2, 4)), dma((2, 2, 4)), dma((2, 2, 4)), dma((2, 4)), dma((2, 4)),
             dma((4,)), dma((4,)), dma((2,)), dma((2,)), dma((4,)), dma((4,)), dma((2,)), dma((2,)),
-            dma((4, 2)), dma((8,)),
+            dma((4, 2, HOME_PARTS)), dma((8, HOME_PARTS)),
         ],
         compiler_params=pltpu.CompilerParams(
-            collective_id=0, has_side_effects=True, vmem_limit_bytes=56 * 2**20
+            collective_id=0, has_side_effects=True, vmem_limit_bytes=48 * 2**20
         ),
         cost_estimate=pl.CostEstimate(flops=3 * 2**32, bytes_accessed=20 * 2**20, transcendentals=0),
-    )(grad, momentum, left, right)
-
-
-def per_device(grad, momentum, variance, weight, left_inverse, right_inverse):
-    precond = precondition(grad, momentum, left_inverse, right_inverse)
-    momentum_next = first_decay * momentum + (1.0 - first_decay) * grad.astype(jnp.float32)
-    variance_next = second_decay * variance + (1.0 - second_decay) * precond * precond
-    weight_float = weight.astype(jnp.float32)
-    weight_next = weight_float - learn_rate * (
-        precond / (jnp.sqrt(variance_next) + epsilon) + weight_decay * weight_float
-    )
-    return (momentum_next, variance_next, weight_next.astype(jnp.bfloat16))
+    )(grad, momentum, variance, weight, left, right)
+    return pl.pallas_call(
+        store,
+        out_shape=[jax.ShapeDtypeStruct(x.shape, x.dtype) for x in updated],
+        in_specs=[pl.BlockSpec(memory_space=pl.ANY)] * 3,
+        out_specs=[pl.BlockSpec(memory_space=pl.ANY)] * 3,
+        scratch_shapes=[dma((3, 4))],
+        compiler_params=pltpu.CompilerParams(vmem_limit_bytes=2**20),
+    )(*updated)
 
 
 def solution(mesh):
@@ -383,5 +447,5 @@
         P(None, "z", ("y", "a", "h", "k"), None),
     )
     return jax.shard_map(
-        per_device, mesh=torus, in_specs=in_specs, out_specs=(tiles, tiles, tiles), check_vma=False
+        update, mesh=torus, in_specs=in_specs, out_specs=(tiles, tiles, tiles), check_vma=False
     )

time: 136 us -> 131 us (0.963); the launches traced: 136 us -> 129 us
  other arithmetic: 8.92 us -> 0 us
  Pallas kernels: 126 us -> 128 us
    convert_element_type x1 -> x0, other arithmetic: 6.11 us -> none  [per_device(): return (momentum_next, variance_next, weight_next.astype(jnp.bfloat16))]
    add x1 -> x0, other arithmetic: 2.81 us -> none  [per_device(): first_decay * momentum + (1.0 - first_decay) * grad.astype(jnp.float32)]
    pallas_call x1 -> x2, Pallas kernels: 126 us -> 128 us  [the longest x1 124 us: update(): pl.pallas_call(kernel, out_shape=(pltpu.VMEM((8, 128, 1024), f32), pltpu....]
where the time goes in v3:
time: 131 us; the launch traced here: 129 us
  Pallas kernels  128 us (98%)
    pallas_call x1, Pallas kernels, update(): pl.pallas_call(kernel, out_shape=(pltpu.VMEM((8, 128, 1024), f32), pltpu....  124 us
    pallas_call x1, Pallas kernels, update(): pl.pallas_call(store, out_shape=[jax.ShapeDtypeStruct(x.shape, x.dtype) f...  4.03 us

profile of v3, /device:TPU:1, one launch (start us, length us, event | category | flops | bytes accessed | tf_op | source)
XLA Modules:
  0.0 128.6 jit_solution(15066780776533338041)
XLA Ops:
  0.6 123.9 %shard_map.85 = (f32[8,128,1024]{2,1,0:T(8,128)S(1)}, f32[8,128,1024]{2,1,0:T(8,128)S(1)}, bf16[8,128,1024]{2,1,0:T(8,128)(2,1)S(1)}) custom-call(bf16[8,128,1024]{2,1,0:T(8,128)(2,1)} %grad.1, f32[8,128,1024]{2,1,0:T(8,128)} %momentum.1, f32[8,128,1024]{2,1,0:T(8,128)} %variance.1, bf16[8,128,1024]{2,1,0:T(8,128)(2,1)} %weight.1, f32[2,32,1024]{2,1,0:T(8,128)} %left.1, ...), custom_call_target="tpu_custom_call" | custom-call | flops 12884901888 | bytes 20971520 | tf_op jit(solution)/shard_map/pallas_call | solution.py:391
  124.6 4.0 %shard_map.86 = (f32[8,128,1024]{2,1,0:T(8,128)}, f32[8,128,1024]{2,1,0:T(8,128)}, bf16[8,128,1024]{2,1,0:T(8,128)(2,1)}) custom-call(f32[8,128,1024]{2,1,0:T(8,128)S(1)} %get-tuple-element.6.momentum, f32[8,128,1024]{2,1,0:T(8,128)S(1)} %get-tuple-element.7.variance, bf16[8,128,1024]{2,1,0:T(8,128)(2,1)S(1)} %get-tuple-element.8.weight), custom_call_target="tpu_custom_call" | custom-call | tf_op jit(solution)/shard_map/pallas_call | solution.py:428

commit v4 on v3

--- a/solution.py
+++ b/solution.py
@@ -64,15 +64,16 @@
         packs.append(pltpu.make_async_copy(right.at[:, 0, :, columns], right_own.at[:, :, packed], pack_sem.at[1, d]))
     for copy in packs:
         copy.start()
-    loads = []
-    for b in range(8):
-        pair = (
+    order = [(dy, t) for dy in (2, 1, 3, 0) for t in range(2)]
+    loads = {}
+    for dy, t in order:
+        b = 2 * step(y, dy) + t
+        loads[dy, t] = (
             pltpu.make_async_copy(momentum.at[b], own.at[b], in_sem.at[0, b]),
             pltpu.make_async_copy(grad.at[b], grad_in.at[b], in_sem.at[1, b]),
         )
-        for copy in pair:
+        for copy in loads[dy, t]:
             copy.start()
-        loads.append(pair)
     late = [
         pltpu.make_async_copy(variance, variance_out, late_sem.at[0]),
         pltpu.make_async_copy(weight, weight_out, late_sem.at[1]),
@@ -94,16 +95,7 @@
         others.append((y, a, h, k, step(z, dz)))
     for device in others:
         pl.semaphore_signal(barrier, inc=1, device_id=device, device_id_type=MESH)
-    for b in range(8):
-        for copy in loads[b]:
-            copy.wait()
-
-        @pl.loop(0, 4)
-        def _(i):
-            rows = pl.ds(pl.multiple_of(i * 32, 32), 32)
-            own[b, rows] = first_decay * own[b, rows] + (1.0 - first_decay) * grad_in[b, rows].astype(jnp.float32)
-
-    for copy in packs + late:
+    for copy in packs:
         copy.wait()
     pl.semaphore_wait(barrier, len(others))
 
@@ -147,24 +139,32 @@
             (to_y, k, h, jnp.int32(t), z),
         )
 
-    def send_part(part):
-        for dy in (2, 1, 3, 0):
-            for t in range(2):
-                src, dst, send, recv, device = own_part(dy, t, part)
-                if dy == 0:
-                    stays = jnp.logical_and(a == k, k == t)
-
-                    @pl.when(stays)
-                    def _():
-                        pltpu.make_async_copy(src, dst, recv).start()
-
-                    @pl.when(jnp.logical_not(stays))
-                    def _():
-                        remote(src, dst, send, recv, device).start()
-                else:
-                    remote(src, dst, send, recv, device).start()
-
-    send_part(0)
+    def send_part(part, dy, t):
+        src, dst, send, recv, device = own_part(dy, t, part)
+        if dy == 0:
+            stays = jnp.logical_and(a == k, k == t)
+
+            @pl.when(stays)
+            def _():
+                pltpu.make_async_copy(src, dst, recv).start()
+
+            @pl.when(jnp.logical_not(stays))
+            def _():
+                remote(src, dst, send, recv, device).start()
+        else:
+            remote(src, dst, send, recv, device).start()
+
+    for dy, t in order:
+        b = 2 * step(y, dy) + t
+        for copy in loads[dy, t]:
+            copy.wait()
+
+        @pl.loop(0, 4)
+        def _(i):
+            rows = pl.ds(pl.multiple_of(i * 32, 32), 32)
+            own[b, rows] = first_decay * own[b, rows] + (1.0 - first_decay) * grad_in[b, rows].astype(jnp.float32)
+
+        send_part(0, dy, t)
 
     def l2(i, from_y):
         rows = left_all.at[from_y, a, z]
@@ -180,6 +180,18 @@
     def l4(s, from_y):
         rows = left_all.at[from_y, s, step(z, 2 * s - 1)]
         return remote(rows, rows, l4_send.at[s, from_y], l4_recv.at[s, from_y], (y, a, h, k, step(z, 1 - 2 * s)))
+
+    def r2(s):
+        rows = right_all.at[y, :, :, k]
+        return remote(rows, rows, r2_send.at[s], r2_recv.at[s], (step(y, 1 - 2 * s), a, h, k, z))
+
+    def r3(dy):
+        rows = right_all.at[step(y, -dy), :, :, k]
+        return remote(rows, rows, r3_send.at[dy], r3_recv.at[dy], (y, a, h, 1 - k, z))
+
+    def r4(s):
+        rows = right_all.at[step(y, 2 * s - 1), s, :, k]
+        return remote(rows, rows, r4_send.at[s], r4_recv.at[s], (step(y, 1 - 2 * s), a, h, k, z))
 
     @pl.when(holder)
     def _():
@@ -191,24 +203,14 @@
             for s in range(2):
                 l3(a, s, from_y).start()
 
-    def r2(s):
-        rows = right_all.at[y, :, :, k]
-        return remote(rows, rows, r2_send.at[s], r2_recv.at[s], (step(y, 1 - 2 * s), a, h, k, z))
-
-    def r3(dy):
-        rows = right_all.at[step(y, -dy), :, :, k]
-        return remote(rows, rows, r3_send.at[dy], r3_recv.at[dy], (y, a, h, 1 - k, z))
-
-    def r4(s):
-        rows = right_all.at[step(y, 2 * s - 1), s, :, k]
-        return remote(rows, rows, r4_send.at[s], r4_recv.at[s], (step(y, 1 - 2 * s), a, h, k, z))
-
     for i in range(4):
         arrived(right_all.at[y, lax.rem(a + i % 2, 2), lax.rem(h + i // 2, 2), k], r1_recv.at[i])
     for s in range(2):
         r2(s).start()
     r3(0).start()
-    send_part(1)
+    for part in range(1, PARTS):
+        for dy, t in order:
+            send_part(part, dy, t)
     for dy in (0, 1, 3, 2):
         from_y = step(y, dy)
 
@@ -221,9 +223,6 @@
         arrived(left_all.at[from_y, 1 - a, z], l2_recv.at[1 - a, from_y])
         for s in range(2):
             l3(1 - a, s, from_y).start()
-    for part in range(2, PARTS):
-        send_part(part)
-
     for s in range(2):
         arrived(right_all.at[step(y, 2 * s - 1), :, :, k], r2_recv.at[s])
         r4(s).start()
@@ -317,6 +316,8 @@
                 else:
                     remote(src, dst, send, recv, device).start()
 
+    for copy in late:
+        copy.wait()
     for dy in (2, 1, 3, 0):
         for t in range(2):
             b = 2 * step(y, -dy) + t

time: 131 us -> 129 us (0.985); the launches traced: 129 us -> 128 us
  no operation moved by 1% of the time
where the time goes in v4:
time: 129 us; the launch traced here: 128 us
  Pallas kernels  127 us (98%)
    pallas_call x1, Pallas kernels, update(): pl.pallas_call(kernel, out_shape=(pltpu.VMEM((8, 128, 1024), f32), pltpu....  123 us
    pallas_call x1, Pallas kernels, update(): pl.pallas_call(store, out_shape=[jax.ShapeDtypeStruct(x.shape, x.dtype) f...  4.03 us

profile of v4, /device:TPU:1, one launch (start us, length us, event | category | flops | bytes accessed | tf_op | source)
XLA Modules:
  0.0 128.0 jit_solution(9722403676380526612)
XLA Ops:
  0.6 123.3 %shard_map.85 = (f32[8,128,1024]{2,1,0:T(8,128)S(1)}, f32[8,128,1024]{2,1,0:T(8,128)S(1)}, bf16[8,128,1024]{2,1,0:T(8,128)(2,1)S(1)}) custom-call(bf16[8,128,1024]{2,1,0:T(8,128)(2,1)} %grad.1, f32[8,128,1024]{2,1,0:T(8,128)} %momentum.1, f32[8,128,1024]{2,1,0:T(8,128)} %variance.1, bf16[8,128,1024]{2,1,0:T(8,128)(2,1)} %weight.1, f32[2,32,1024]{2,1,0:T(8,128)} %left.1, ...), custom_call_target="tpu_custom_call" | custom-call | flops 12884901888 | bytes 20971520 | tf_op jit(solution)/shard_map/pallas_call | solution.py:392
  123.9 4.0 %shard_map.86 = (f32[8,128,1024]{2,1,0:T(8,128)}, f32[8,128,1024]{2,1,0:T(8,128)}, bf16[8,128,1024]{2,1,0:T(8,128)(2,1)}) custom-call(f32[8,128,1024]{2,1,0:T(8,128)S(1)} %get-tuple-element.6.momentum, f32[8,128,1024]{2,1,0:T(8,128)S(1)} %get-tuple-element.7.variance, bf16[8,128,1024]{2,1,0:T(8,128)(2,1)S(1)} %get-tuple-element.8.weight), custom_call_target="tpu_custom_call" | custom-call | tf_op jit(solution)/shard_map/pallas_call | solution.py:429

commit v5 on v4

--- a/solution.py
+++ b/solution.py
@@ -47,6 +47,9 @@
 
     def step(at, by):
         return lax.rem(at + by + 4, 4)
+
+    def plane(dy):
+        return step(y, dy * (1 - 2 * k))
 
     def remote(src, dst, send, recv, device):
         return pltpu.make_async_remote_copy(
@@ -67,7 +70,7 @@
     order = [(dy, t) for dy in (2, 1, 3, 0) for t in range(2)]
     loads = {}
     for dy, t in order:
-        b = 2 * step(y, dy) + t
+        b = 2 * plane(dy) + t
         loads[dy, t] = (
             pltpu.make_async_copy(momentum.at[b], own.at[b], in_sem.at[0, b]),
             pltpu.make_async_copy(grad.at[b], grad_in.at[b], in_sem.at[1, b]),
@@ -129,7 +132,7 @@
         r1(i).start()
 
     def own_part(dy, t, part):
-        to_y = step(y, dy)
+        to_y = plane(dy)
         columns = pl.ds(part * WIDE, WIDE)
         return (
             own.at[2 * to_y + t, :, columns],
@@ -155,7 +158,7 @@
             remote(src, dst, send, recv, device).start()
 
     for dy, t in order:
-        b = 2 * step(y, dy) + t
+        b = 2 * plane(dy) + t
         for copy in loads[dy, t]:
             copy.wait()
 
@@ -278,7 +281,7 @@
                 left_rows(pl.ds(pl.multiple_of(i * 256, 256), 256), columns)
 
     def p_copy(dy, to_a, part):
-        to_y = step(y, dy)
+        to_y = plane(dy)
         columns = pl.ds(part * HOME_WIDE, HOME_WIDE)
         return (
             done.at[2 * to_y + to_a, :, columns],
@@ -289,7 +292,7 @@
         )
 
     for dy in (2, 1, 3, 0):
-        to_y = step(y, dy)
+        to_y = plane(dy)
         rows = pl.ds(pl.multiple_of(to_y * 256, 256), 256)
         left_rows(rows, columns)
         for part in range(HOME_PARTS):
@@ -320,7 +323,7 @@
         copy.wait()
     for dy in (2, 1, 3, 0):
         for t in range(2):
-            b = 2 * step(y, -dy) + t
+            b = 2 * step(y, dy * (2 * t - 1)) + t
             for part in range(HOME_PARTS):
                 columns = pl.ds(part * HOME_WIDE, HOME_WIDE)
                 arrived(home_tile.at[b, :, columns], p_recv.at[b, part])

time: 129 us -> 132 us (1.023)
  the two profiles are of different devices: /device:TPU:1 before, /device:TPU:26 now
where the time goes in v5:
time: 132 us
  Pallas kernels  131 us (99%)
    pallas_call x1, Pallas kernels, update(): pl.pallas_call(kernel, out_shape=(pltpu.VMEM((8, 128, 1024), f32), pltpu....  127 us
    pallas_call x1, Pallas kernels, update(): pl.pallas_call(store, out_shape=[jax.ShapeDtypeStruct(x.shape, x.dtype) f...  4.03 us

profile of v5, /device:TPU:26, one launch (start us, length us, event | category | flops | bytes accessed | tf_op | source)
XLA Modules:
  0.0 131.8 jit_solution(9563905538256695840)
XLA Ops:
  0.6 127.2 %shard_map.85 = (f32[8,128,1024]{2,1,0:T(8,128)S(1)}, f32[8,128,1024]{2,1,0:T(8,128)S(1)}, bf16[8,128,1024]{2,1,0:T(8,128)(2,1)S(1)}) custom-call(bf16[8,128,1024]{2,1,0:T(8,128)(2,1)} %grad.1, f32[8,128,1024]{2,1,0:T(8,128)} %momentum.1, f32[8,128,1024]{2,1,0:T(8,128)} %variance.1, bf16[8,128,1024]{2,1,0:T(8,128)(2,1)} %weight.1, f32[2,32,1024]{2,1,0:T(8,128)} %left.1, ...), custom_call_target="tpu_custom_call" | custom-call | flops 12884901888 | bytes 20971520 | tf_op jit(solution)/shard_map/pallas_call | solution.py:395
  127.8 4.0 %shard_map.86 = (f32[8,128,1024]{2,1,0:T(8,128)}, f32[8,128,1024]{2,1,0:T(8,128)}, bf16[8,128,1024]{2,1,0:T(8,128)(2,1)}) custom-call(f32[8,128,1024]{2,1,0:T(8,128)S(1)} %get-tuple-element.6.momentum, f32[8,128,1024]{2,1,0:T(8,128)S(1)} %get-tuple-element.7.variance, bf16[8,128,1024]{2,1,0:T(8,128)(2,1)S(1)} %get-tuple-element.8.weight), custom_call_target="tpu_custom_call" | custom-call | tf_op jit(solution)/shard_map/pallas_call | solution.py:432
